TPU v7x, 128 devices: a whole 4x4x4 slice. The times are simulated.
128 devices in a mesh: slide: 4 (over y), gy: 4 (over z), gx: 8 (over x, core).
Axes of the slice: x: 4, y: 4, z: 4, core: 2. Of those that a mesh axis runs over, the one named last changes fastest.
Arguments:
- feature_map: bfloat16 [2048, 1024, 256], P(('slide', 'gy'), 'gx'), parts along dimension 0, may hold values from -6 to 6
- depth_kernel: float32 [7, 7, 256], replicated, may hold values from -0.875 to 0.875
- depth_bias: float32 [256], replicated, may hold values from -3 to 3
- norm_gain: float32 [256], replicated, may hold values from 0.1 to 1.9
- norm_bias: float32 [256], replicated, may hold values from -3 to 3
- up_weight: bfloat16 [256, 1024], replicated, may hold values from -0.375 to 0.375
- up_bias: float32 [1024], replicated, may hold values from -3 to 3
- down_weight: bfloat16 [1024, 256], replicated, may hold values from -0.1875 to 0.1875
- down_bias: float32 [256], replicated, may hold values from -3 to 3
- layer_scale: float32 [256], replicated, may hold values from 0.5 to 1.5
- tile_route: int32 [128, 96], P(('slide', 'gy', 'gx')), parts along dimension 0, may hold values from -1 to 127, as said below
Outputs:
- balanced_tiles: bfloat16 [6144, 128, 256], P(('slide', 'gy', 'gx')), parts along dimension 0
There are 4 independent parts, one for each index of `slide`. A program takes and returns all parts, laid end to end along the dimension named above; an argument that names none is the same for every part. Nothing has to cross between parts.
Inputs may be any that keep to these rules, and one draw needn't show every extreme that they name: `tile_route`: each entry is a tile index of the sending device or -1. Every device's listed tiles are distinct, one device lists exactly 96 tiles and none more, and the entries that are not -1 for one receiver number at most 48, exactly 48 for some receiver.
All inputs are finite; a program needn't handle non-finite values.
Results may differ from a plain program's by a relative error of at most 0.0049.
Values may be sent and summed in bfloat16 or wider, within the bound.
A program may use at most 192 MiB of HBM per device.

v0:
```python
import jax
import jax.numpy as jnp
from jax import lax
from jax.sharding import PartitionSpec as P

RECV = 48


def extended_2(cells, sides, width):
    for axis, dim in sides:
        count = lax.axis_size(axis)
        ends = count - 1
        head = lax.slice_in_dim(cells, 0, width, axis=dim)
        tail = lax.slice_in_dim(cells, cells.shape[dim] - width, cells.shape[dim], axis=dim)
        cells = jnp.concatenate(
            [
                lax.ppermute(tail, axis, [(i, (i + 1) % count) for i in range(ends)]),
                cells,
                lax.ppermute(head, axis, [((i + 1) % count, i) for i in range(ends)]),
            ],
            axis=dim,
        )
    return cells


def pointwise(
    x_tiles, dw_tiles, norm_gain, norm_bias, up_weight, up_bias, down_weight, down_bias, layer_scale
):
    rows = dw_tiles.reshape(-1, dw_tiles.shape[-1]).astype(jnp.float32)
    center = jnp.mean(rows, axis=1, keepdims=True)
    spread = jnp.mean((rows - center) ** 2, axis=1, keepdims=True)
    normed = ((rows - center) / jnp.sqrt(spread + 1e-06) * norm_gain + norm_bias).astype(
        jnp.bfloat16
    )
    hidden = jnp.dot(normed, up_weight, preferred_element_type=jnp.float32) + up_bias
    hidden = jax.nn.gelu(hidden, approximate=False).astype(jnp.bfloat16)
    branch = jnp.dot(hidden, down_weight, preferred_element_type=jnp.float32) + down_bias
    result = x_tiles.reshape(-1, x_tiles.shape[-1]).astype(jnp.float32) + layer_scale * branch
    return result.astype(jnp.bfloat16).reshape(x_tiles.shape)


def depthwise_sum(padded, depth_kernel, depth_bias, rows, cols):
    total = jnp.zeros((rows, cols, padded.shape[2]), jnp.float32) + depth_bias
    for first in range(depth_kernel.shape[0]):
        for second in range(depth_kernel.shape[1]):
            window = padded[first : first + rows, second : second + cols].astype(jnp.float32)
            total = total + depth_kernel[first, second] * window
    return total.astype(jnp.bfloat16)


def deliver(stacked, route_row):
    return (
        lax.all_to_all(stacked, ("gy", "gx"), split_axis=0, concat_axis=0, tiled=True),
        lax.all_to_all(route_row, ("gy", "gx"), split_axis=0, concat_axis=0, tiled=True),
    )


def compact_slots(received_row, stacked):
    count = received_row.shape[0]
    live = (received_row >= 0).astype(jnp.int32)
    rank = jnp.cumsum(live) - 1
    slot_ids = jnp.arange(RECV, dtype=jnp.int32)
    select = ((rank[None, :] == slot_ids[:, None]) & (live[None, :] > 0)).astype(jnp.int32)
    source = jnp.sum(select * jnp.arange(count, dtype=jnp.int32)[None, :], axis=1)
    valid = jnp.sum(select, axis=1) > 0
    return (jnp.take(stacked, source, axis=0), valid)


def per_device(
    feature_map,
    depth_kernel,
    depth_bias,
    norm_gain,
    norm_bias,
    up_weight,
    up_bias,
    down_weight,
    down_bias,
    layer_scale,
    tile_route,
):
    width = depth_kernel.shape[0] // 2
    extended = extended_2(feature_map, (("gy", 0), ("gx", 1)), width)
    depthwise = depthwise_sum(
        extended, depth_kernel, depth_bias, feature_map.shape[0], feature_map.shape[1]
    )
    route_row = tile_route[0]
    safe = jnp.maximum(route_row, 0)
    x_send = jnp.take(feature_map, safe, axis=0)
    dw_send = jnp.take(depthwise, safe, axis=0)
    params = (norm_gain, norm_bias, up_weight, up_bias, down_weight, down_bias, layer_scale)
    result = pointwise(x_send, dw_send, *params)
    got, got_row = deliver(result[:, None], route_row)
    picked, valid = compact_slots(got_row, got)
    output = picked[:, 0]
    return jnp.where(valid[:, None, None], output, jnp.zeros_like(output))


def solution(mesh):
    in_specs = (
        P(("slide", "gy"), "gx", None),
        P(),
        P(),
        P(),
        P(),
        P(),
        P(),
        P(),
        P(),
        P(),
        P(("slide", "gy", "gx"), None),
    )
    out_specs = P(("slide", "gy", "gx"), None, None)
    return jax.shard_map(
        per_device, mesh=mesh, in_specs=in_specs, out_specs=out_specs, check_vma=False
    )
```

profile of v0, /device:TPU:1, one launch (start us, length us, event | category | flops | bytes accessed | tf_op | source)
XLA Modules:
  0.0 530.0 jit_solution(11324954977440964184)
XLA Ops:
  0.0 1.1 fusion.106
  1.1 4.4 collective-permute-start
  5.5 1.3 collective-permute-start.1
  7.3 1.3 reduce.13
  9.4 9.7 %all-to-all-start = ((s32[32,3,1]{1,2,0:T(1,128)}), s32[32,3,1]{1,2,0:T(1,128)}, u32[]{:S(2)}, u32[]{:S(2)}) async-start(s32[32,3,1]{1,2,0:T(1,128)} %bitcast), calls=%async_computation | async-start | bytes 32768 | tf_op jit(solution)/shard_map/all_to_all | solution.py:54
  19.7 1.0 fusion.107
  20.7 9.4 %gather_fusion.1 = bf16[96,128,256]{2,1,0:T(8,128)(2,1)} fusion(bf16[128,128,256]{2,1,0:T(8,128)(2,1)} %param.13, s32[1024]{0:T(1024)S(1)} %pad_clamp_fusion.1), kind=kCustom, calls=%fused_computation.clone | custom fusion | bytes 12583296 | tf_op jit(solution)/shard_map/jit(_take)/gather | solution.py:89
  30.8 10.6 %constant_dynamic-update-slice_fusion.3 = (bf16[131,128,256]{2,1,0:T(8,128)(2,1)}, bf16[134,128,256]{2,1,0:T(8,128)(2,1)S(1)}, bf16[131,128,256]{2,1,0:T(8,128)(2,1)}) fusion(bf16[131,128,256]{2,1,0:T(8,128)(2,1)} %get-tuple-element.17, bf16[128,128,256]{2,1,0:T(8,128)(2,1)} %param.13, bf16[134,128,256]{2,1,0:T(8,128)(2,1)S(1)} %get-tuple-element.18), kind=kLoop, calls=%fused_computation.146 | loop fusion | bytes 33554432 | tf_op jit(solution)/shard_map/concatenate | solution.py:15
  42.1 3.4 copy-done.2
  45.8 2.2 collective-permute-start.3
  48.0 3.6 collective-permute-start.2
  51.6 1.3 collective-permute-done.3
  53.0 1.1 collective-permute-done.2
  54.2 225.7 %add_convert_fusion = bf16[128,128,256]{2,1,0:T(8,128)(2,1)} fusion(bf16[128,128,256]{2,1,0:T(8,128)(2,1)} %param.13, bf16[134,3,256]{2,1,0:T(4,128)(2,1)S(1)} %copy.35, bf16[134,3,256]{2,1,0:T(4,128)(2,1)S(1)} %copy.33, bf16[134,128,256]{2,1,0:T(8,128)(2,1)} %copy-done.2, bf16[131,128,256]{2,1,0:T(8,128)(2,1)} %get-tuple-element.19, ...), kind=kLoop, calls=%fused_computation.66 | loop fusion | flops 1149239296 | bytes 76353536 | tf_op jit(solution)/shard_map/convert_element_type | solution.py:48
  279.9 9.4 %gather_fusion.2 = bf16[96,128,256]{2,1,0:T(8,128)(2,1)} fusion(bf16[128,128,256]{2,1,0:T(8,128)(2,1)} %add_convert_fusion, s32[1024]{0:T(1024)S(1)} %pad_clamp_fusion.1), kind=kCustom, calls=%fused_computation.1.clone | custom fusion | bytes 12583296 | tf_op jit(solution)/shard_map/jit(_take)/gather | solution.py:90
  289.4 4.7 fusion.104
  294.1 8.6 %select_convert_fusion = (f32[96,128,256]{2,1,0:T(8,128)S(1)}, bf16[96,128,256]{2,1,0:T(8,128)(2,1)}) fusion(bf16[96,128,256]{2,1,0:T(8,128)(2,1)} %gather_fusion.2, pred[96]{0:T(512)(128)(4,1)S(1)} %get-tuple-element.8, bf16[96,128,256]{2,1,0:T(8,128)(2,1)} %gather_fusion.1), kind=kLoop, calls=%fused_computation.131 | loop fusion | flops 9437184 | bytes 31457376 | tf_op jit(solution)/shard_map/convert_element_type | solution.py:29
  302.9 4.4 multiply_reduce_fusion
  307.4 11.4 %fusion.27 = bf16[12288,256]{1,0:T(8,128)(2,1)} fusion(f32[96,128,256]{2,1,0:T(8,128)S(1)} %get-tuple-element.72, f32[256]{0:T(256)S(1)} %copy-done.5, f32[256]{0:T(256)S(1)} %copy-done.6, f32[12288]{0:T(1024)S(1)} %sqrt_bitcast_fusion, f32[12288]{0:T(1024)S(1)} %get-tuple-element.70), kind=kLoop, calls=%fused_computation.73 | loop fusion | flops 15728640 | bytes 18974720 | tf_op jit(solution)/shard_map/convert_element_type | solution.py:32
  318.8 120.0 %fusion.21 = bf16[12288,256]{1,0:T(8,128)(2,1)} fusion(bf16[1024,256]{1,0:T(8,128)(2,1)S(1)} %copy-done, f32[1024]{0:T(1024)S(1)} %copy-done.8, bf16[12288,256]{1,0:T(8,128)(2,1)} %bitcast.88, bf16[12288,256]{1,0:T(8,128)(2,1)} %fusion.27, bf16[256,1024]{1,0:T(8,128)(2,1)S(1)} %copy-done.7, f32[256]{0:T(256)S(1)} %copy-done.9, f32[256]{0:T(256)S(1)} %copy-done.10), kind=kOutput, calls=%fused_computation.67 | convolution fusion | flops 13731102720 | bytes 19929088 | tf_op jit(solution)/shard_map/dot_general | solution.py:37
  438.8 8.6 %all-to-all-start.1 = ((bf16[96,1,128,256]{3,2,1,0:T(8,128)(2,1)}), bf16[96,1,128,256]{3,2,1,0:T(8,128)(2,1)}, u32[]{:S(2)}, u32[]{:S(2)}) async-start(bf16[96,1,128,256]{3,2,1,0:T(8,128)(2,1)} %bitcast.87), calls=%async_computation.1 | async-start | bytes 12582912 | tf_op jit(solution)/shard_map/all_to_all | solution.py:53
  449.5 70.8 %all-to-all-done.1 = bf16[96,1,128,256]{3,2,1,0:T(8,128)(2,1)} async-done(((bf16[96,1,128,256]{3,2,1,0:T(8,128)(2,1)}), bf16[96,1,128,256]{3,2,1,0:T(8,128)(2,1)}, u32[]{:S(2)}, u32[]{:S(2)}) %all-to-all-start.1) | async-done | bytes 6291488 | tf_op jit(solution)/shard_map/all_to_all | solution.py:53
  520.3 5.3 %gather_fusion = bf16[48,128,256]{2,1,0:T(8,128)(2,1)} fusion(bf16[96,128,256]{2,1,0:T(8,128)(2,1)} %bitcast.57, s32[1024]{0:T(1024)S(1)} %pad_clamp_fusion), kind=kCustom, calls=%fused_computation.2 | custom fusion | bytes 6291648 | tf_op jit(solution)/shard_map/jit(_take)/gather | solution.py:66
  525.6 4.0 select_select_fusion
  (54 shorter events, 6.0 us)
Async XLA Ops:
  0.0 318.8 %copy-start = (bf16[1024,256]{1,0:T(8,128)(2,1)S(1)}, bf16[1024,256]{1,0:T(8,128)(2,1)}, u32[]{:S(2)}) copy-start(bf16[1024,256]{1,0:T(8,128)(2,1)} %param.20) | copy-start | bytes 1572868
  0.0 30.1 %copy-start.3 = (f32[7,7,256]{2,1,0:T(8,128)S(1)}, f32[7,7,256]{2,1,0:T(8,128)}, u32[]{:S(2)}) copy-start(f32[7,7,256]{2,1,0:T(8,128)} %param.14) | copy-start | bytes 150532
  1.1 29.0 %collective-permute-start = (bf16[3,128,256]{2,1,0:T(8,128)(2,1)S(1)}, bf16[3,128,256]{2,1,0:T(8,128)(2,1)S(1)}, u32[]{:S(2)}, u32[]{:S(2)}) collective-permute-start(bf16[3,128,256]{2,1,0:T(8,128)(2,1)S(1)} %get-tuple-element.16), channel_id=1, source_target_pairs={{0,8},{8,16},{16,24},{1,9},{9,17},{17,25},{2,10},{10,18},{18,26},{... | collective-permute-start | bytes 589832 | tf_op jit(solution)/shard_map/ppermute | solution.py:17
  5.5 35.9 %collective-permute-start.1 = (bf16[3,128,256]{2,1,0:T(8,128)(2,1)S(1)}, bf16[3,128,256]{2,1,0:T(8,128)(2,1)S(1)}, u32[]{:S(2)}, u32[]{:S(2)}) collective-permute-start(bf16[3,128,256]{2,1,0:T(8,128)(2,1)S(1)} %get-tuple-element.15), channel_id=1, source_target_pairs={{8,0},{16,8},{24,16},{9,1},{17,9},{25,17},{10,2},{18,10},{26,18},{... | collective-permute-start | bytes 589832 | tf_op jit(solution)/shard_map/ppermute | solution.py:19
  9.4 429.4 %all-to-all-start = ((s32[32,3,1]{1,2,0:T(1,128)}), s32[32,3,1]{1,2,0:T(1,128)}, u32[]{:S(2)}, u32[]{:S(2)}) async-start(s32[32,3,1]{1,2,0:T(1,128)} %bitcast), calls=%async_computation | async-start | bytes 32768 | tf_op jit(solution)/shard_map/all_to_all | solution.py:54
  30.8 23.4 %copy-start.4 = (f32[256]{0:T(256)S(1)}, f32[256]{0:T(256)}, u32[]{:S(2)}) copy-start(f32[256]{0:T(256)} %param.15) | copy-start | bytes 3076
  42.1 3.4 copy-start.2
  45.8 7.1 %collective-permute-start.3 = (bf16[134,3,256]{2,0,1:T(8,128)(2,1)S(1)}, bf16[134,3,256]{2,0,1:T(8,128)(2,1)S(1)}, u32[]{:S(2)}, u32[]{:S(2)}) collective-permute-start(bf16[134,3,256]{2,0,1:T(8,128)(2,1)S(1)} %copy.34), channel_id=1, source_target_pairs={{1,0},{2,1},{3,2},{4,3},{5,4},{6,5},{7,6},{9,8},{10,9},{11,10},{12... | collective-permute-start | bytes 617480 | tf_op jit(solution)/shard_map/ppermute | solution.py:19
  48.0 6.1 %collective-permute-start.2 = (bf16[134,3,256]{2,0,1:T(8,128)(2,1)S(1)}, bf16[134,3,256]{2,0,1:T(8,128)(2,1)S(1)}, u32[]{:S(2)}, u32[]{:S(2)}) collective-permute-start(bf16[134,3,256]{2,0,1:T(8,128)(2,1)S(1)} %copy.32), channel_id=1, source_target_pairs={{0,1},{1,2},{2,3},{3,4},{4,5},{5,6},{6,7},{8,9},{9,10},{10,11},{11... | collective-permute-start | bytes 617480 | tf_op jit(solution)/shard_map/ppermute | solution.py:17
  289.3 13.4 %slice-start = ((s8[6291456]{0:T(1024)(128)(4,1)}), s8[2097152]{0:T(1024)(128)(4,1)S(1)}, s32[]{:S(2)}) async-start(s8[6291456]{0:T(1024)(128)(4,1)} %bitcast.85), calls=%async_computation.2 | async-start | bytes 4194304
  294.1 8.7 %slice-start.1 = ((s8[6291456]{0:T(1024)(128)(4,1)}), s8[4194304]{0:T(1024)(128)(4,1)S(1)}, s32[]{:S(2)}) async-start(s8[6291456]{0:T(1024)(128)(4,1)} %bitcast.85), calls=%async_computation.3 | async-start | bytes 8388608
  294.1 13.2 %copy-start.5 = (f32[256]{0:T(256)S(1)}, f32[256]{0:T(256)}, u32[]{:S(2)}) copy-start(f32[256]{0:T(256)} %param.17) | copy-start | bytes 3076
  294.1 13.2 %copy-start.6 = (f32[256]{0:T(256)S(1)}, f32[256]{0:T(256)}, u32[]{:S(2)}) copy-start(f32[256]{0:T(256)} %param.16) | copy-start | bytes 3076
  302.8 15.9 %copy-start.7 = (bf16[256,1024]{1,0:T(8,128)(2,1)S(1)}, bf16[256,1024]{1,0:T(8,128)(2,1)}, u32[]{:S(2)}) copy-start(bf16[256,1024]{1,0:T(8,128)(2,1)} %param.18) | copy-start | bytes 1572868
  302.8 15.9 %copy-start.8 = (f32[1024]{0:T(1024)S(1)}, f32[1024]{0:T(1024)}, u32[]{:S(2)}) copy-start(f32[1024]{0:T(1024)} %param.19) | copy-start | bytes 12292
  302.8 15.9 %copy-start.9 = (f32[256]{0:T(256)S(1)}, f32[256]{0:T(256)}, u32[]{:S(2)}) copy-start(f32[256]{0:T(256)} %param.21) | copy-start | bytes 3076
  302.9 15.9 %copy-start.10 = (f32[256]{0:T(256)S(1)}, f32[256]{0:T(256)}, u32[]{:S(2)}) copy-start(f32[256]{0:T(256)} %param.22) | copy-start | bytes 3076
  438.8 90.8 %copy-start.1 = (bf16[1024,256]{1,0:T(8,128)(2,1)S(1)}, bf16[1024,256]{1,0:T(8,128)(2,1)}, u32[]{:S(2)}) copy-start(bf16[1024,256]{1,0:T(8,128)(2,1)} %param.20) | copy-start | bytes 1572868
  438.8 81.5 %all-to-all-start.1 = ((bf16[96,1,128,256]{3,2,1,0:T(8,128)(2,1)}), bf16[96,1,128,256]{3,2,1,0:T(8,128)(2,1)}, u32[]{:S(2)}, u32[]{:S(2)}) async-start(bf16[96,1,128,256]{3,2,1,0:T(8,128)(2,1)} %bitcast.87), calls=%async_computation.1 | async-start | bytes 12582912 | tf_op jit(solution)/shard_map/all_to_all | solution.py:53
where the time goes:
time: 538 us; the launch traced here: 530 us
  other arithmetic  263 us (49%)
  matrix products  120 us (22%)
  waiting for transfers between devices  73.2 us (14%)
  local copies, waits for them, and re-layouts  43.6 us (8%)
  starting transfers between devices  29.6 us (6%)
    convert_element_type x1, other arithmetic, depthwise_sum(): return total.astype(jnp.bfloat16)  226 us
    dot_general x1, matrix products, pointwise(): jnp.dot(hidden, down_weight, preferred_element_type=jnp.float32) + down_bias  120 us
    all_to_all x1, waiting for transfers between devices, deliver(): lax.all_to_all(stacked, ('gy', 'gx'), split_axis=0, concat_axis=0, tiled=...  70.8 us
    convert_element_type x1, other arithmetic, pointwise(): ((rows - center) / jnp.sqrt(spread + 1e-06) * norm_gain + norm_bias).asty...  11.4 us
    concatenate x2, local copies, waits for them, and re-layouts, extended_2(): jnp.concatenate([lax.ppermute(tail, axis, [(i, (i + 1) % count) for i in...  11.3 us
  transfers between devices with their start and end apart: 6, of which 3 were waited for; matrix products, arithmetic and copies ran while one was open for 78% of the time, Pallas kernels for 0%

commit v1 on v0

v1 whole, which is shorter than its diff:
```python
import functools

import jax
import jax.numpy as jnp
import numpy as np
from jax import lax
from jax.experimental import pallas as pl
from jax.experimental.pallas import tpu as pltpu
from jax.sharding import PartitionSpec as P

B16 = jnp.bfloat16
F32 = jnp.float32
MESH = pl.DeviceIdType.MESH
GY, GX = 4, 8
N = GY * GX
SLOT = 3
RECV = 48
ROWS, COLS, C = 128, 128, 256
HID = 1024
EXT = COLS + 16
KS = 7


def shift_matrix():
    s = np.zeros((COLS, KS * EXT), np.float32)
    for b in range(KS):
        for j in range(COLS):
            s[j, b * EXT + (j + b - 3) % EXT] = 1.0
    return s


def pack_matrices():
    first = np.zeros((64, 256), np.float32)
    last = np.zeros((64, 256), np.float32)
    for u in range(16):
        for c in range(4):
            first[u * 4 + c, u * 16 + c] = 1.0
            last[u * 4 + c, u * 16 + 12 + c] = 1.0
    return first, last


def unpack_matrices():
    left = np.zeros((256, 64), np.float32)
    right = np.zeros((256, 64), np.float32)
    for u in range(16):
        for c in range(3):
            right[u * 16 + c, u * 4 + c] = 1.0
            left[u * 16 + 13 + c, u * 4 + 1 + c] = 1.0
    return left, right


def corner_matrix():
    m = np.zeros((96, 64), np.float32)
    for r in range(3):
        for c in range(3):
            m[r * 16 + 13 + c, (r + 1) * 4 + 1 + c] = 1.0
            m[r * 16 + c, 16 + (r + 1) * 4 + c] = 1.0
            m[48 + r * 16 + 13 + c, 32 + r * 4 + 1 + c] = 1.0
            m[48 + r * 16 + c, 48 + r * 4 + c] = 1.0
    return m


def conv_tile(xp, kb, row, pp):
    for h in range(2):
        ls = slice(h * 128, (h + 1) * 128)
        for bs in ((0, 1, 2, 3), (4, 5, 6)):
            w = {(a, b): kb[a * KS + b, :, ls] for a in range(KS) for b in bs}

            def block(blk, _):
                o = pl.multiple_of(blk * 16, 16)
                xs = [xp[row + a, pl.ds(o, 16), ls] for a in range(KS)]
                for b in bs:
                    q = [xs[a] * w[(a, b)] for a in range(KS)]
                    s = ((q[0] + q[1]) + (q[2] + q[3])) + ((q[4] + q[5]) + q[6])
                    pp[pl.ds(b * EXT + o, 16), ls] = s
                return 0

            lax.fori_loop(0, EXT // 16, block, 0, unroll=True)


def order(k):
    i, j = k // GY, k % GY
    dy = jnp.where(j == 0, 2, jnp.where(j == 1, 1, jnp.where(j == 2, 3, 0)))
    half = (i + 1) // 2
    dx = (4 + jnp.where(i % 2 == 1, -half, half)) % GX
    return dy, dx


def block_kernel(
    route, x, sroute, kern, smat, pf, plast, ul, ur, cm, dbias, gain, nbias, uw, ub, dw, db, scale,
    recv, routes,
    xp, kb, pp, stage, hsend, hrecv, corner,
    xsem, rows_s, rows_r, cols_s, cols_r, cor_s, cor_r, rt_s, rt_r, send_s, recv_s, own_s,
):
    sl = lax.axis_index("slide")
    gy = lax.axis_index("gy")
    gx = lax.axis_index("gx")
    me = gy * GX + gx

    def dev(y, z):
        return (sl, y, z)

    load = pltpu.make_async_copy(x, xp.at[pl.ds(3, ROWS), pl.ds(0, COLS)], xsem)
    load.start()

    barrier = pltpu.get_barrier_semaphore()

    def greet(k, _):
        r = (me + 1 + k) % N
        pl.semaphore_signal(barrier, inc=1, device_id=dev(r // GX, r % GX), device_id_type=MESH)
        return 0

    lax.fori_loop(0, N - 1, greet, 0)

    def weights(i, _):
        kb[i] = jnp.broadcast_to(kern[i], (16, C)).astype(B16)
        return 0

    lax.fori_loop(0, KS * KS, weights, 0)
    load.wait()

    def pack(q, _):
        lo = xp[pl.ds(3 + q * 16, 16), 0:16, :].reshape(256, C)
        hi = xp[pl.ds(3 + q * 16, 16), COLS - 16 : COLS, :].reshape(256, C)
        hsend[0, q] = jnp.dot(pf[...], lo, preferred_element_type=F32).astype(B16)
        hsend[1, q] = jnp.dot(plast[...], hi, preferred_element_type=F32).astype(B16)
        return 0

    lax.fori_loop(0, 8, pack, 0)
    pl.semaphore_wait(barrier, N - 1)

    up, down = (gy + GY - 1) % GY, (gy + 1) % GY
    left, right = (gx + GX - 1) % GX, (gx + 1) % GX

    def remote(src, dst, s, r, where):
        return pltpu.make_async_remote_copy(
            src_ref=src, dst_ref=dst, send_sem=s, recv_sem=r, device_id=where, device_id_type=MESH
        )

    halo = [
        remote(hsend.at[0], hrecv.at[1], cols_s.at[0], cols_r.at[1], dev(gy, left)),
        remote(hsend.at[1], hrecv.at[0], cols_s.at[1], cols_r.at[0], dev(gy, right)),
        remote(x.at[pl.ds(0, 3)], xp.at[pl.ds(ROWS + 3, 3), pl.ds(0, COLS)], rows_s.at[0], rows_r.at[1], dev(up, gx)),
        remote(x.at[pl.ds(ROWS - 3, 3)], xp.at[pl.ds(0, 3), pl.ds(0, COLS)], rows_s.at[1], rows_r.at[0], dev(down, gx)),
        remote(hsend.at[1, 7, pl.ds(48, 16)], corner.at[pl.ds(0, 16)], cor_s.at[0], cor_r.at[0], dev(down, right)),
        remote(hsend.at[0, 7, pl.ds(48, 16)], corner.at[pl.ds(16, 16)], cor_s.at[1], cor_r.at[1], dev(down, left)),
        remote(hsend.at[1, 0, pl.ds(0, 16)], corner.at[pl.ds(32, 16)], cor_s.at[2], cor_r.at[2], dev(up, right)),
        remote(hsend.at[0, 0, pl.ds(0, 16)], corner.at[pl.ds(48, 16)], cor_s.at[3], cor_r.at[3], dev(up, left)),
    ]
    for h in halo:
        h.start()
    for h in halo:
        h.wait()

    @pl.when(gx == 0)
    def _():
        hrecv[0] = jnp.zeros_like(hrecv[0])
        corner[0:16] = jnp.zeros((16, C), B16)
        corner[32:48] = jnp.zeros((16, C), B16)

    @pl.when(gx == GX - 1)
    def _():
        hrecv[1] = jnp.zeros_like(hrecv[1])
        corner[16:32] = jnp.zeros((16, C), B16)
        corner[48:64] = jnp.zeros((16, C), B16)

    @pl.when(gy == 0)
    def _():
        xp[0:3, 0:COLS] = jnp.zeros((3, COLS, C), B16)
        corner[0:32] = jnp.zeros((32, C), B16)

    @pl.when(gy == GY - 1)
    def _():
        xp[ROWS + 3 : ROWS + 6, 0:COLS] = jnp.zeros((3, COLS, C), B16)
        corner[32:64] = jnp.zeros((32, C), B16)

    def unpack(q, _):
        both = jnp.dot(ul[...], hrecv[0, q], preferred_element_type=F32) + jnp.dot(
            ur[...], hrecv[1, q], preferred_element_type=F32
        )
        xp[pl.ds(3 + q * 16, 16), COLS:EXT, :] = both.astype(B16).reshape(16, 16, C)
        return 0

    lax.fori_loop(0, 8, unpack, 0)
    edge = jnp.dot(cm[...], corner[...], preferred_element_type=F32).astype(B16).reshape(2, 3, 16, C)
    xp[0:3, COLS:EXT, :] = edge[0]
    xp[ROWS + 3 : ROWS + 6, COLS:EXT, :] = edge[1]

    def place(k):
        dy, dx = order(k)
        return (gy + dy) % GY, (gx + dx) % GX

    def tell(k, _):
        ry, rx = place(k)
        remote(sroute.at[ry * GX + rx], routes.at[me], rt_s, rt_r, dev(ry, rx)).start()
        return 0

    lax.fori_loop(0, N - 1, tell, 0)

    def compute(k):
        ry, rx = place(k)
        r = ry * GX + rx
        rows = [jnp.maximum(route[0, r * SLOT + t], 0) for t in range(SLOT)]
        normed = []
        for t in range(SLOT):
            conv_tile(xp, kb, rows[t], pp.at[t])
        for t in range(SLOT):
            d = jnp.dot(smat[...], pp[t], preferred_element_type=F32) + dbias[...]
            c = d - jnp.mean(d, axis=1, keepdims=True)
            v = jnp.mean(c * c, axis=1, keepdims=True)
            normed.append((c * lax.rsqrt(v + 1e-6) * gain[...] + nbias[...]).astype(B16))
        n = jnp.concatenate(normed, axis=0)
        branch = None
        for q in range(4):
            qs = slice(q * 256, (q + 1) * 256)
            hh = jnp.dot(n, uw[:, qs], preferred_element_type=F32) + ub[:, qs]
            g = (0.5 * hh * (1.0 + lax.erf(hh * 0.7071067811865476))).astype(B16)
            part = jnp.dot(g, dw[qs, :], preferred_element_type=F32)
            branch = part if branch is None else branch + part
        branch = branch + db[...]
        for t in range(SLOT):
            o = xp[rows[t] + 3, 0:COLS, :].astype(F32) + scale[...] * branch[t * COLS : (t + 1) * COLS]
            stage[k, t] = o.astype(B16)
        return ry, rx

    def step(k, _):
        ry, rx = compute(k)

        @pl.when(k < N - 1)
        def _():
            remote(stage.at[k], recv.at[me], send_s.at[k], recv_s.at[me], dev(ry, rx)).start()

        @pl.when(k == N - 1)
        def _():
            pltpu.make_async_copy(stage.at[k], recv.at[me], own_s.at[0]).start()

        return 0

    lax.fori_loop(0, N, step, 0)
    mine = pltpu.make_async_copy(sroute.at[me], routes.at[me], own_s.at[1])
    mine.start()
    mine.wait()
    pltpu.make_async_copy(stage.at[N - 1], recv.at[me], own_s.at[0]).wait()
    several = routes.at[pl.ds(0, N - 1)]
    pltpu.make_async_copy(several, several, rt_s).wait()
    pltpu.make_async_copy(several, several, rt_r).wait()

    def finish(k, _):
        s = (me + 1 + k) % N
        here = remote(stage.at[k], recv.at[s], send_s.at[k], recv_s.at[s], dev(gy, gx))
        here.wait_send()
        here.wait_recv()
        return 0

    lax.fori_loop(0, N - 1, finish, 0)


def compact_kernel(routes, recv, out, zero, sem):
    zero[...] = jnp.zeros_like(zero)

    def look(i, count):
        v = routes[i // SLOT, 0, i % SLOT]
        take = jnp.logical_and(v >= 0, count < RECV)

        @pl.when(take)
        def _():
            pltpu.make_async_copy(recv.at[i // SLOT, i % SLOT], out.at[count], sem).start()

        return count + take.astype(jnp.int32)

    count = lax.fori_loop(0, N * SLOT, look, jnp.int32(0))

    def blank(k, _):
        pltpu.make_async_copy(zero, out.at[k], sem).start()
        return 0

    lax.fori_loop(count, RECV, blank, 0)
    pltpu.make_async_copy(out, out, sem).wait()


def per_device(
    feature_map, depth_kernel, depth_bias, norm_gain, norm_bias, up_weight, up_bias, down_weight, down_bias,
    layer_scale, tile_route,
):
    vm = pl.BlockSpec(memory_space=pltpu.VMEM)
    anym = pl.BlockSpec(memory_space=pl.ANY)
    smem = pl.BlockSpec(memory_space=pltpu.SMEM)
    sroute = jnp.pad(tile_route.reshape(N, 1, SLOT), ((0, 0), (0, 0), (0, 128 - SLOT)), constant_values=-1)
    pf, plast = pack_matrices()
    ul, ur = unpack_matrices()
    const = [jnp.asarray(m, B16) for m in (shift_matrix(), pf, plast, ul, ur, corner_matrix())]
    row = lambda a: a.reshape(1, -1)
    dma = pltpu.SemaphoreType.DMA
    recv, routes = pl.pallas_call(
        block_kernel,
        out_shape=(
            jax.ShapeDtypeStruct((N, SLOT, COLS, C), B16),
            jax.ShapeDtypeStruct((N, 1, 128), jnp.int32),
        ),
        in_specs=[smem, anym, anym] + [vm] * 15,
        out_specs=(anym, anym),
        scratch_shapes=[
            pltpu.VMEM((ROWS + 6, EXT, C), B16),
            pltpu.VMEM((KS * KS, 16, C), B16),
            pltpu.VMEM((SLOT, KS * EXT, C), B16),
            pltpu.VMEM((N, SLOT, COLS, C), B16),
            pltpu.VMEM((2, 8, 64, C), B16),
            pltpu.VMEM((2, 8, 64, C), B16),
            pltpu.VMEM((64, C), B16),
            dma,
            dma((2,)), dma((2,)), dma((2,)), dma((2,)), dma((4,)), dma((4,)),
            dma, dma, dma((N,)), dma((N,)), dma((2,)),
        ],
        compiler_params=pltpu.CompilerParams(
            collective_id=0, has_side_effects=True, vmem_limit_bytes=56 * 2**20
        ),
    )(
        tile_route, feature_map, sroute, depth_kernel.reshape(KS * KS, 1, C), *const, row(depth_bias),
        row(norm_gain), row(norm_bias), up_weight, row(up_bias), down_weight, row(down_bias), row(layer_scale),
    )
    return pl.pallas_call(
        compact_kernel,
        out_shape=jax.ShapeDtypeStruct((RECV, COLS, C), B16),
        in_specs=[smem, anym],
        out_specs=anym,
        scratch_shapes=[pltpu.VMEM((COLS, C), B16), dma],
    )(routes, recv)


def solution(mesh):
    in_specs = (P(("slide", "gy"), "gx", None),) + (P(),) * 9 + (P(("slide", "gy", "gx"), None),)
    out_specs = P(("slide", "gy", "gx"), None, None)
    return jax.shard_map(per_device, mesh=mesh, in_specs=in_specs, out_specs=out_specs, check_vma=False)
```

time: 538 us -> 227 us (0.42)
  other arithmetic: 263 us -> 1.32 us
  Pallas kernels: 0 us -> 219 us
  matrix products: 120 us -> 0 us
  waiting for transfers between devices: 73.2 us -> 0 us
  local copies, waits for them, and re-layouts: 43.6 us -> 2.71 us
  starting transfers between devices: 29.6 us -> 0 us
    convert_element_type x4 -> x0, other arithmetic: 247 us -> none  [the longest x1 226 us: depthwise_sum(): return total.astype(jnp.bfloat16)]
    pallas_call x0 -> x2, Pallas kernels: none -> 219 us  [the longest x1 122 us: per_device(): pl.pallas_call(block_kernel, out_shape=(jax.ShapeDtypeStruct((N, SLOT, CO...]
    dot_general x1 -> x0, matrix products: 120 us -> none  [pointwise(): jnp.dot(hidden, down_weight, preferred_element_type=jnp.float32) + down_bias]
    all_to_all x2 -> x0, waiting for transfers between devices: 70.8 us -> none  [the longest x1 70.8 us: deliver(): lax.all_to_all(stacked, ('gy', 'gx'), split_axis=0, concat_axis=0, tiled=...]
    gather x3 -> x0, local copies, waits for them, and re-layouts: 24.1 us -> none  [the longest x1 9.4 us: per_device(): dw_send = jnp.take(depthwise, safe, axis=0)]
    all_to_all x2 -> x0, starting transfers between devices: 18.2 us -> none  [the longest x1 9.66 us: deliver(): lax.all_to_all(route_row, ('gy', 'gx'), split_axis=0, concat_axis=0, tile...]
    ppermute x4 -> x0, starting transfers between devices: 11.4 us -> none  [the longest x2 7.96 us: extended_2(): lax.ppermute(tail, axis, [(i, (i + 1) % count) for i in range(ends)])]
    concatenate x2 -> x0, local copies, waits for them, and re-layouts: 11.3 us -> none  [extended_2(): jnp.concatenate([lax.ppermute(tail, axis, [(i, (i + 1) % count) for i in...]
  transfers between devices with their start and end apart: 6 -> 0, of which waited for: 3 -> 0; matrix products, arithmetic and copies ran while one was open for 78% -> 0% of each run, Pallas kernels for 0% -> 0%
where the time goes in v1:
time: 227 us; the launch traced here: 223 us
  Pallas kernels  219 us (96%)
  local copies, waits for them, and re-layouts  2.71 us (1%)
    pallas_call x1, Pallas kernels, per_device(): pl.pallas_call(block_kernel, out_shape=(jax.ShapeDtypeStruct((N, SLOT, CO...  122 us
    pallas_call x1, Pallas kernels, per_device(): pl.pallas_call(compact_kernel, out_shape=jax.ShapeDtypeStruct((RECV, COLS...  97.3 us

profile of v1, /device:TPU:1, one launch (start us, length us, event | category | flops | bytes accessed | tf_op | source)
XLA Modules:
  0.0 223.2 jit_solution(15443262632785847537)
XLA Ops:
  0.0 0.5 broadcast.5
  0.5 1.3 reduce.3
  1.8 0.1 reshape.24
  1.9 0.6 pad.4.sroute
  2.5 1.5 reshape.25.kern
  4.0 121.8 %shard_map.163 = (bf16[32,3,128,256]{3,2,1,0:T(8,128)(2,1)}, s32[32,1,128]{2,1,0:T(1,128)}) custom-call(s32[1,96]{1,0:T(1,128)} %route.1, bf16[128,128,256]{2,1,0:T(8,128)(2,1)} %x.3, s32[32,1,128]{2,1,0:T(1,128)} %pad.4.sroute, f32[49,1,256]{2,1,0:T(1,128)} %reshape.25.kern, bf16[128,1008]{1,0:T(8,128)(2,1)} %constant.14.clone.smat, ...), custom_call_target="tpu_custom_call" | custom-call | tf_op jit(solution)/shard_map/pallas_call | solution.py:294
  125.9 97.3 %shard_map.164 = bf16[48,128,256]{2,1,0:T(8,128)(2,1)} custom-call(s32[32,1,128]{2,1,0:T(1,128)} %get-tuple-element.7.routes, bf16[32,3,128,256]{3,2,1,0:T(8,128)(2,1)} %get-tuple-element.8.recv), custom_call_target="tpu_custom_call" | custom-call | tf_op jit(solution)/shard_map/pallas_call | solution.py:321

commit v2 on v1

--- a/solution.py
+++ b/solution.py
@@ -60,30 +60,32 @@
     return m
 
 
-def conv_tile(xp, kb, row, pp):
-    for h in range(2):
-        ls = slice(h * 128, (h + 1) * 128)
-        for bs in ((0, 1, 2, 3), (4, 5, 6)):
-            w = {(a, b): kb[a * KS + b, :, ls] for a in range(KS) for b in bs}
-
-            def block(blk, _):
-                o = pl.multiple_of(blk * 16, 16)
-                xs = [xp[row + a, pl.ds(o, 16), ls] for a in range(KS)]
+GROUPS = ((0, 1, 2), (3, 4), (5, 6))
+STEPS = (
+    (2, 2), (1, 1), (3, 3), (2, 0), (0, 2), (1, 3), (3, 1), (2, 1),
+    (1, 0), (2, 3), (3, 0), (1, 2), (0, 1), (3, 2), (0, 3), (0, 0),
+)
+
+
+def conv_group(xp, kb, rows, pp):
+    for bs in GROUPS:
+        w = {(a, b): kb[a * KS + b] for a in range(KS) for b in bs}
+
+        def block(blk, _):
+            o = pl.multiple_of(blk * 16, 16)
+            for t, row in enumerate(rows):
+                xs = [xp[row + a, pl.ds(o, 16), :] for a in range(KS)]
                 for b in bs:
                     q = [xs[a] * w[(a, b)] for a in range(KS)]
                     s = ((q[0] + q[1]) + (q[2] + q[3])) + ((q[4] + q[5]) + q[6])
-                    pp[pl.ds(b * EXT + o, 16), ls] = s
-                return 0
-
-            lax.fori_loop(0, EXT // 16, block, 0, unroll=True)
-
-
-def order(k):
-    i, j = k // GY, k % GY
-    dy = jnp.where(j == 0, 2, jnp.where(j == 1, 1, jnp.where(j == 2, 3, 0)))
-    half = (i + 1) // 2
-    dx = (4 + jnp.where(i % 2 == 1, -half, half)) % GX
-    return dy, dx
+                    pp[t, pl.ds(b * EXT + o, 16), :] = s
+            return 0
+
+        lax.fori_loop(0, EXT // 16, block, 0)
+
+
+def look_up(k, table):
+    return sum(jnp.where(k == i, v, 0) for i, v in enumerate(table))
 
 
 def block_kernel(
@@ -112,22 +114,9 @@
 
     lax.fori_loop(0, N - 1, greet, 0)
 
-    def weights(i, _):
-        kb[i] = jnp.broadcast_to(kern[i], (16, C)).astype(B16)
-        return 0
-
-    lax.fori_loop(0, KS * KS, weights, 0)
-    load.wait()
-
-    def pack(q, _):
-        lo = xp[pl.ds(3 + q * 16, 16), 0:16, :].reshape(256, C)
-        hi = xp[pl.ds(3 + q * 16, 16), COLS - 16 : COLS, :].reshape(256, C)
-        hsend[0, q] = jnp.dot(pf[...], lo, preferred_element_type=F32).astype(B16)
-        hsend[1, q] = jnp.dot(plast[...], hi, preferred_element_type=F32).astype(B16)
-        return 0
-
-    lax.fori_loop(0, 8, pack, 0)
-    pl.semaphore_wait(barrier, N - 1)
+    for a in range(KS):
+        for b in range(KS):
+            kb[a * KS + b] = jnp.broadcast_to(kern[a, b : b + 1, :], (16, C)).astype(B16)
 
     up, down = (gy + GY - 1) % GY, (gy + 1) % GY
     left, right = (gx + GX - 1) % GX, (gx + 1) % GX
@@ -137,19 +126,48 @@
             src_ref=src, dst_ref=dst, send_sem=s, recv_sem=r, device_id=where, device_id_type=MESH
         )
 
-    halo = [
+    halo_rows = [
+        remote(x.at[pl.ds(0, 3)], xp.at[pl.ds(ROWS + 3, 3), pl.ds(0, COLS)], rows_s.at[0], rows_r.at[1], dev(up, gx)),
+        remote(x.at[pl.ds(ROWS - 3, 3)], xp.at[pl.ds(0, 3), pl.ds(0, COLS)], rows_s.at[1], rows_r.at[0], dev(down, gx)),
+    ]
+    halo_cols = [
         remote(hsend.at[0], hrecv.at[1], cols_s.at[0], cols_r.at[1], dev(gy, left)),
         remote(hsend.at[1], hrecv.at[0], cols_s.at[1], cols_r.at[0], dev(gy, right)),
-        remote(x.at[pl.ds(0, 3)], xp.at[pl.ds(ROWS + 3, 3), pl.ds(0, COLS)], rows_s.at[0], rows_r.at[1], dev(up, gx)),
-        remote(x.at[pl.ds(ROWS - 3, 3)], xp.at[pl.ds(0, 3), pl.ds(0, COLS)], rows_s.at[1], rows_r.at[0], dev(down, gx)),
         remote(hsend.at[1, 7, pl.ds(48, 16)], corner.at[pl.ds(0, 16)], cor_s.at[0], cor_r.at[0], dev(down, right)),
         remote(hsend.at[0, 7, pl.ds(48, 16)], corner.at[pl.ds(16, 16)], cor_s.at[1], cor_r.at[1], dev(down, left)),
         remote(hsend.at[1, 0, pl.ds(0, 16)], corner.at[pl.ds(32, 16)], cor_s.at[2], cor_r.at[2], dev(up, right)),
         remote(hsend.at[0, 0, pl.ds(0, 16)], corner.at[pl.ds(48, 16)], cor_s.at[3], cor_r.at[3], dev(up, left)),
     ]
-    for h in halo:
+
+    pl.semaphore_wait(barrier, N - 1)
+    for h in halo_rows:
         h.start()
-    for h in halo:
+    load.wait()
+    for q in range(8):
+        lo = xp[3 + q * 16 : 19 + q * 16, 0:16, :].reshape(256, C)
+        hi = xp[3 + q * 16 : 19 + q * 16, COLS - 16 : COLS, :].reshape(256, C)
+        hsend[0, q] = jnp.dot(pf[...], lo, preferred_element_type=F32).astype(B16)
+        hsend[1, q] = jnp.dot(plast[...], hi, preferred_element_type=F32).astype(B16)
+    for h in halo_cols:
+        h.start()
+
+    def place(k):
+        core, cx = gx % 2, gx // 2
+        c, t = k // 2, k % 2
+        a, b = look_up(c, [o[0] for o in STEPS]), look_up(c, [o[1] for o in STEPS])
+        dy, dx = jnp.where(core == 0, a, b), jnp.where(core == 0, b, a)
+        return (gy + dy) % GY, ((cx + dx) % (GX // 2)) * 2 + (core + 1 + t) % 2
+
+    def tell(k, _):
+        ry, rx = place(k)
+        remote(sroute, routes.at[me], rt_s, rt_r, dev(ry, rx)).start()
+        return 0
+
+    lax.fori_loop(0, N - 1, tell, 0)
+    mine = pltpu.make_async_copy(sroute, routes.at[me], own_s.at[1])
+    mine.start()
+
+    for h in halo_cols:
         h.wait()
 
     @pl.when(gx == 0)
@@ -166,44 +184,38 @@
 
     @pl.when(gy == 0)
     def _():
-        xp[0:3, 0:COLS] = jnp.zeros((3, COLS, C), B16)
         corner[0:32] = jnp.zeros((32, C), B16)
 
     @pl.when(gy == GY - 1)
     def _():
-        xp[ROWS + 3 : ROWS + 6, 0:COLS] = jnp.zeros((3, COLS, C), B16)
         corner[32:64] = jnp.zeros((32, C), B16)
 
-    def unpack(q, _):
+    for q in range(8):
         both = jnp.dot(ul[...], hrecv[0, q], preferred_element_type=F32) + jnp.dot(
             ur[...], hrecv[1, q], preferred_element_type=F32
         )
-        xp[pl.ds(3 + q * 16, 16), COLS:EXT, :] = both.astype(B16).reshape(16, 16, C)
-        return 0
-
-    lax.fori_loop(0, 8, unpack, 0)
+        xp[3 + q * 16 : 19 + q * 16, COLS:EXT, :] = both.astype(B16).reshape(16, 16, C)
     edge = jnp.dot(cm[...], corner[...], preferred_element_type=F32).astype(B16).reshape(2, 3, 16, C)
     xp[0:3, COLS:EXT, :] = edge[0]
     xp[ROWS + 3 : ROWS + 6, COLS:EXT, :] = edge[1]
 
-    def place(k):
-        dy, dx = order(k)
-        return (gy + dy) % GY, (gx + dx) % GX
-
-    def tell(k, _):
-        ry, rx = place(k)
-        remote(sroute.at[ry * GX + rx], routes.at[me], rt_s, rt_r, dev(ry, rx)).start()
-        return 0
-
-    lax.fori_loop(0, N - 1, tell, 0)
+    for h in halo_rows:
+        h.wait()
+
+    @pl.when(gy == 0)
+    def _():
+        xp[0:3, 0:COLS] = jnp.zeros((3, COLS, C), B16)
+
+    @pl.when(gy == GY - 1)
+    def _():
+        xp[ROWS + 3 : ROWS + 6, 0:COLS] = jnp.zeros((3, COLS, C), B16)
 
     def compute(k):
         ry, rx = place(k)
         r = ry * GX + rx
         rows = [jnp.maximum(route[0, r * SLOT + t], 0) for t in range(SLOT)]
         normed = []
-        for t in range(SLOT):
-            conv_tile(xp, kb, rows[t], pp.at[t])
+        conv_group(xp, kb, rows, pp)
         for t in range(SLOT):
             d = jnp.dot(smat[...], pp[t], preferred_element_type=F32) + dbias[...]
             c = d - jnp.mean(d, axis=1, keepdims=True)
@@ -237,8 +249,6 @@
         return 0
 
     lax.fori_loop(0, N, step, 0)
-    mine = pltpu.make_async_copy(sroute.at[me], routes.at[me], own_s.at[1])
-    mine.start()
     mine.wait()
     pltpu.make_async_copy(stage.at[N - 1], recv.at[me], own_s.at[0]).wait()
     several = routes.at[pl.ds(0, N - 1)]
@@ -255,27 +265,37 @@
     lax.fori_loop(0, N - 1, finish, 0)
 
 
-def compact_kernel(routes, recv, out, zero, sem):
-    zero[...] = jnp.zeros_like(zero)
+def compact_kernel(routes, recv, out, held, in_s, out_s):
+    me = lax.axis_index("gy") * GX + lax.axis_index("gx")
 
     def look(i, count):
-        v = routes[i // SLOT, 0, i % SLOT]
+        v = routes[i // SLOT, 0, me * SLOT + i % SLOT]
         take = jnp.logical_and(v >= 0, count < RECV)
 
         @pl.when(take)
         def _():
-            pltpu.make_async_copy(recv.at[i // SLOT, i % SLOT], out.at[count], sem).start()
+            pltpu.make_async_copy(recv.at[i // SLOT, i % SLOT], held.at[count], in_s.at[count]).start()
 
         return count + take.astype(jnp.int32)
 
     count = lax.fori_loop(0, N * SLOT, look, jnp.int32(0))
 
     def blank(k, _):
-        pltpu.make_async_copy(zero, out.at[k], sem).start()
+        held[k] = jnp.zeros((COLS, C), B16)
         return 0
 
     lax.fori_loop(count, RECV, blank, 0)
-    pltpu.make_async_copy(out, out, sem).wait()
+
+    def pass_on(k, _):
+        @pl.when(k < count)
+        def _():
+            pltpu.make_async_copy(recv.at[0, 0], held.at[k], in_s.at[k]).wait()
+
+        pltpu.make_async_copy(held.at[k], out.at[k], out_s).start()
+        return 0
+
+    lax.fori_loop(0, RECV, pass_on, 0)
+    pltpu.make_async_copy(held, out, out_s).wait()
 
 
 def per_device(
@@ -285,7 +305,6 @@
     vm = pl.BlockSpec(memory_space=pltpu.VMEM)
     anym = pl.BlockSpec(memory_space=pl.ANY)
     smem = pl.BlockSpec(memory_space=pltpu.SMEM)
-    sroute = jnp.pad(tile_route.reshape(N, 1, SLOT), ((0, 0), (0, 0), (0, 128 - SLOT)), constant_values=-1)
     pf, plast = pack_matrices()
     ul, ur = unpack_matrices()
     const = [jnp.asarray(m, B16) for m in (shift_matrix(), pf, plast, ul, ur, corner_matrix())]
@@ -295,7 +314,7 @@
         block_kernel,
         out_shape=(
             jax.ShapeDtypeStruct((N, SLOT, COLS, C), B16),
-            jax.ShapeDtypeStruct((N, 1, 128), jnp.int32),
+            jax.ShapeDtypeStruct((N, 1, N * SLOT), jnp.int32),
         ),
         in_specs=[smem, anym, anym] + [vm] * 15,
         out_specs=(anym, anym),
@@ -315,7 +334,7 @@
             collective_id=0, has_side_effects=True, vmem_limit_bytes=56 * 2**20
         ),
     )(
-        tile_route, feature_map, sroute, depth_kernel.reshape(KS * KS, 1, C), *const, row(depth_bias),
+        tile_route, feature_map, tile_route, depth_kernel, *const, row(depth_bias),
         row(norm_gain), row(norm_bias), up_weight, row(up_bias), down_weight, row(down_bias), row(layer_scale),
     )
     return pl.pallas_call(
@@ -323,7 +342,7 @@
         out_shape=jax.ShapeDtypeStruct((RECV, COLS, C), B16),
         in_specs=[smem, anym],
         out_specs=anym,
-        scratch_shapes=[pltpu.VMEM((COLS, C), B16), dma],
+        scratch_shapes=[pltpu.VMEM((RECV, COLS, C), B16), dma((RECV,)), dma],
     )(routes, recv)
 
 

time: 227 us -> 102 us (0.45); the launches traced: 223 us -> 102 us
  Pallas kernels: 219 us -> 102 us
  local copies, waits for them, and re-layouts: 2.71 us -> 0 us
    pallas_call x1, Pallas kernels: 97.3 us -> 4.92 us  [per_device(): pl.pallas_call(compact_kernel, out_shape=jax.ShapeDtypeStruct((RECV, COLS...]
    pallas_call x1, Pallas kernels: 122 us -> 97 us  [per_device(): pl.pallas_call(block_kernel, out_shape=(jax.ShapeDtypeStruct((N, SLOT, CO...]
where the time goes in v2:
time: 102 us
  Pallas kernels  102 us (100%)
    pallas_call x1, Pallas kernels, per_device(): pl.pallas_call(block_kernel, out_shape=(jax.ShapeDtypeStruct((N, SLOT, CO...  97 us
    pallas_call x1, Pallas kernels, per_device(): pl.pallas_call(compact_kernel, out_shape=jax.ShapeDtypeStruct((RECV, COLS...  4.92 us

profile of v2, /device:TPU:1, one launch (start us, length us, event | category | flops | bytes accessed | tf_op | source)
XLA Modules:
  0.0 101.9 jit_solution(10258974100877362294)
XLA Ops:
  0.0 97.0 %shard_map.163 = (bf16[32,3,128,256]{3,2,1,0:T(8,128)(2,1)}, s32[32,1,96]{2,1,0:T(1,128)}) custom-call(s32[1,96]{1,0:T(1,128)} %sroute.1, bf16[128,128,256]{2,1,0:T(8,128)(2,1)} %x.1, s32[1,96]{1,0:T(1,128)} %sroute.1, f32[7,7,256]{2,1,0:T(8,128)} %kern.1, bf16[128,1008]{1,0:T(8,128)(2,1)} %constant.12.clone.smat, bf16[64,256]{1,0:T(8,128)(2,1)} %constant.13.clone.pf, ...), custom_call_target="tpu_custom_call" | custom-call | tf_op jit(solution)/shard_map/pallas_call | solution.py:313
  97.0 4.9 %shard_map.164 = bf16[48,128,256]{2,1,0:T(8,128)(2,1)} custom-call(s32[32,1,96]{2,1,0:T(1,128)} %get-tuple-element.7.routes, bf16[32,3,128,256]{3,2,1,0:T(8,128)(2,1)} %get-tuple-element.8.recv), custom_call_target="tpu_custom_call" | custom-call | tf_op jit(solution)/shard_map/pallas_call | solution.py:340

commit v3 on v2

--- a/solution.py
+++ b/solution.py
@@ -61,10 +61,16 @@
 
 
 GROUPS = ((0, 1, 2), (3, 4), (5, 6))
-STEPS = (
+CHIPS = (
     (2, 2), (1, 1), (3, 3), (2, 0), (0, 2), (1, 3), (3, 1), (2, 1),
-    (1, 0), (2, 3), (3, 0), (1, 2), (0, 1), (3, 2), (0, 3), (0, 0),
+    (1, 0), (2, 3), (3, 0), (1, 2), (0, 1), (3, 2), (0, 3),
 )
+STEPS = tuple(
+    sorted(
+        [(z, x, t) for t in (1, 0) for z, x in CHIPS],
+        key=lambda o: -(o[0] == 2) - (o[1] == 2),
+    )
+) + ((0, 0, 1), (0, 0, 0))
 
 
 def conv_group(xp, kb, rows, pp):
@@ -89,10 +95,10 @@
 
 
 def block_kernel(
-    route, x, sroute, kern, smat, pf, plast, ul, ur, cm, dbias, gain, nbias, uw, ub, dw, db, scale,
+    route, x, sroute, kern, smat_h, pf, plast, ul, ur, cm, dbias, gain, nbias, uw_h, ub, dw_h, db, scale,
     recv, routes,
-    xp, kb, pp, stage, hsend, hrecv, corner,
-    xsem, rows_s, rows_r, cols_s, cols_r, cor_s, cor_r, rt_s, rt_r, send_s, recv_s, own_s,
+    xp, kb, pp, stage, hsend, hrecv, corner, smat, uw, dw,
+    xsem, rows_s, rows_r, cols_s, cols_r, cor_s, cor_r, rt_s, rt_r, send_s, recv_s, own_s, w_s,
 ):
     sl = lax.axis_index("slide")
     gy = lax.axis_index("gy")
@@ -113,6 +119,11 @@
         return 0
 
     lax.fori_loop(0, N - 1, greet, 0)
+    held = [
+        pltpu.make_async_copy(h, v, w_s.at[i]) for i, (h, v) in enumerate(((smat_h, smat), (uw_h, uw), (dw_h, dw)))
+    ]
+    for h in held:
+        h.start()
 
     for a in range(KS):
         for b in range(KS):
@@ -153,10 +164,9 @@
 
     def place(k):
         core, cx = gx % 2, gx // 2
-        c, t = k // 2, k % 2
-        a, b = look_up(c, [o[0] for o in STEPS]), look_up(c, [o[1] for o in STEPS])
+        a, b, t = (look_up(k, [o[i] for o in STEPS]) for i in range(3))
         dy, dx = jnp.where(core == 0, a, b), jnp.where(core == 0, b, a)
-        return (gy + dy) % GY, ((cx + dx) % (GX // 2)) * 2 + (core + 1 + t) % 2
+        return (gy + dy) % GY, ((cx + dx) % (GX // 2)) * 2 + (core + t) % 2
 
     def tell(k, _):
         ry, rx = place(k)
@@ -209,6 +219,9 @@
     @pl.when(gy == GY - 1)
     def _():
         xp[ROWS + 3 : ROWS + 6, 0:COLS] = jnp.zeros((3, COLS, C), B16)
+
+    for h in held:
+        h.wait()
 
     def compute(k):
         ry, rx = place(k)
@@ -240,7 +253,7 @@
 
         @pl.when(k < N - 1)
         def _():
-            remote(stage.at[k], recv.at[me], send_s.at[k], recv_s.at[me], dev(ry, rx)).start()
+            remote(stage.at[k], recv.at[me], send_s, recv_s, dev(ry, rx)).start()
 
         @pl.when(k == N - 1)
         def _():
@@ -255,47 +268,33 @@
     pltpu.make_async_copy(several, several, rt_s).wait()
     pltpu.make_async_copy(several, several, rt_r).wait()
 
-    def finish(k, _):
-        s = (me + 1 + k) % N
-        here = remote(stage.at[k], recv.at[s], send_s.at[k], recv_s.at[s], dev(gy, gx))
-        here.wait_send()
-        here.wait_recv()
-        return 0
-
-    lax.fori_loop(0, N - 1, finish, 0)
-
-
-def compact_kernel(routes, recv, out, held, in_s, out_s):
+    sent = stage.at[pl.ds(0, N - 1)]
+    pltpu.make_async_copy(sent, sent, send_s).wait()
+    pltpu.make_async_copy(sent, sent, recv_s).wait()
+
+
+def compact_kernel(routes, recv, out, zero, sem):
     me = lax.axis_index("gy") * GX + lax.axis_index("gx")
+    zero[...] = jnp.zeros_like(zero)
 
     def look(i, count):
-        v = routes[i // SLOT, 0, me * SLOT + i % SLOT]
-        take = jnp.logical_and(v >= 0, count < RECV)
+        g, s = i // SLOT, i % SLOT
+        take = jnp.logical_and(routes[g, 0, me * SLOT + s] >= 0, count < RECV)
 
         @pl.when(take)
         def _():
-            pltpu.make_async_copy(recv.at[i // SLOT, i % SLOT], held.at[count], in_s.at[count]).start()
+            pltpu.make_async_copy(recv.at[g, s], out.at[count], sem).start()
 
         return count + take.astype(jnp.int32)
 
     count = lax.fori_loop(0, N * SLOT, look, jnp.int32(0))
 
     def blank(k, _):
-        held[k] = jnp.zeros((COLS, C), B16)
+        pltpu.make_async_copy(zero, out.at[k], sem).start()
         return 0
 
     lax.fori_loop(count, RECV, blank, 0)
-
-    def pass_on(k, _):
-        @pl.when(k < count)
-        def _():
-            pltpu.make_async_copy(recv.at[0, 0], held.at[k], in_s.at[k]).wait()
-
-        pltpu.make_async_copy(held.at[k], out.at[k], out_s).start()
-        return 0
-
-    lax.fori_loop(0, RECV, pass_on, 0)
-    pltpu.make_async_copy(held, out, out_s).wait()
+    pltpu.make_async_copy(out, out, sem).wait()
 
 
 def per_device(
@@ -313,11 +312,11 @@
     recv, routes = pl.pallas_call(
         block_kernel,
         out_shape=(
-            jax.ShapeDtypeStruct((N, SLOT, COLS, C), B16),
+            pltpu.VMEM((N, SLOT, COLS, C), B16),
             jax.ShapeDtypeStruct((N, 1, N * SLOT), jnp.int32),
         ),
-        in_specs=[smem, anym, anym] + [vm] * 15,
-        out_specs=(anym, anym),
+        in_specs=[smem, anym, anym, vm, anym] + [vm] * 8 + [anym, vm, anym, vm, vm],
+        out_specs=(vm, anym),
         scratch_shapes=[
             pltpu.VMEM((ROWS + 6, EXT, C), B16),
             pltpu.VMEM((KS * KS, 16, C), B16),
@@ -326,12 +325,15 @@
             pltpu.VMEM((2, 8, 64, C), B16),
             pltpu.VMEM((2, 8, 64, C), B16),
             pltpu.VMEM((64, C), B16),
+            pltpu.VMEM((COLS, KS * EXT), B16),
+            pltpu.VMEM((C, HID), B16),
+            pltpu.VMEM((HID, C), B16),
             dma,
             dma((2,)), dma((2,)), dma((2,)), dma((2,)), dma((4,)), dma((4,)),
-            dma, dma, dma((N,)), dma((N,)), dma((2,)),
+            dma, dma, dma, dma, dma((2,)), dma((3,)),
         ],
         compiler_params=pltpu.CompilerParams(
-            collective_id=0, has_side_effects=True, vmem_limit_bytes=56 * 2**20
+            collective_id=0, has_side_effects=True, vmem_limit_bytes=50 * 2**20
         ),
     )(
         tile_route, feature_map, tile_route, depth_kernel, *const, row(depth_bias),
@@ -340,10 +342,11 @@
     return pl.pallas_call(
         compact_kernel,
         out_shape=jax.ShapeDtypeStruct((RECV, COLS, C), B16),
-        in_specs=[smem, anym],
+        in_specs=[smem, vm],
         out_specs=anym,
-        scratch_shapes=[pltpu.VMEM((RECV, COLS, C), B16), dma((RECV,)), dma],
-    )(routes, recv)
+        scratch_shapes=[pltpu.VMEM((COLS, C), B16), dma],
+        compiler_params=pltpu.CompilerParams(vmem_limit_bytes=50 * 2**20),
+    )(routes, pltpu.with_memory_space_constraint(recv, pltpu.VMEM))
 
 
 def solution(mesh):

time: 102 us -> 97.5 us (0.956)
  Pallas kernels: 102 us -> 96.9 us
    pallas_call x1, Pallas kernels: 97 us -> 93.5 us  [per_device(): pl.pallas_call(block_kernel, out_shape=(pltpu.VMEM((N, SLOT, COLS, C), B1...]
    pallas_call x1, Pallas kernels: 4.92 us -> 3.4 us  [per_device(): pl.pallas_call(compact_kernel, out_shape=jax.ShapeDtypeStruct((RECV, COLS...]
where the time goes in v3:
time: 97.5 us; the launch traced here: 96.9 us
  Pallas kernels  96.9 us (99%)
    pallas_call x1, Pallas kernels, per_device(): pl.pallas_call(block_kernel, out_shape=(pltpu.VMEM((N, SLOT, COLS, C), B1...  93.5 us
    pallas_call x1, Pallas kernels, per_device(): pl.pallas_call(compact_kernel, out_shape=jax.ShapeDtypeStruct((RECV, COLS...  3.4 us

profile of v3, /device:TPU:1, one launch (start us, length us, event | category | flops | bytes accessed | tf_op | source)
XLA Modules:
  0.0 96.9 jit_solution(4821277221574990294)
XLA Ops:
  0.0 93.5 %shard_map.163 = (bf16[32,3,128,256]{3,2,1,0:T(8,128)(2,1)S(1)}, s32[32,1,96]{2,1,0:T(1,128)}) custom-call(s32[1,96]{1,0:T(1,128)} %sroute.1, bf16[128,128,256]{2,1,0:T(8,128)(2,1)} %x.1, s32[1,96]{1,0:T(1,128)} %sroute.1, f32[7,7,256]{2,1,0:T(8,128)} %kern.1, bf16[128,1008]{1,0:T(8,128)(2,1)} %constant.12.clone.smat_h, bf16[64,256]{1,0:T(8,128)(2,1)} %constant.13.clone.pf, ...), custom_call_target="tpu_custom_call" | custom-call | tf_op jit(solution)/shard_map/pallas_call | solution.py:312
  93.5 3.4 %shard_map.164 = bf16[48,128,256]{2,1,0:T(8,128)(2,1)} custom-call(s32[32,1,96]{2,1,0:T(1,128)} %get-tuple-element.7.routes, bf16[32,3,128,256]{3,2,1,0:T(8,128)(2,1)S(1)} %get-tuple-element.8.recv), custom_call_target="tpu_custom_call" | custom-call | tf_op jit(solution)/shard_map/pallas_call | solution.py:342

commit v4 on v3

--- a/solution.py
+++ b/solution.py
@@ -65,12 +65,19 @@
     (2, 2), (1, 1), (3, 3), (2, 0), (0, 2), (1, 3), (3, 1), (2, 1),
     (1, 0), (2, 3), (3, 0), (1, 2), (0, 1), (3, 2), (0, 3),
 )
-STEPS = tuple(
-    sorted(
-        [(z, x, t) for t in (1, 0) for z, x in CHIPS],
-        key=lambda o: -(o[0] == 2) - (o[1] == 2),
-    )
-) + ((0, 0, 1), (0, 0, 0))
+
+
+def steps():
+    every = [(z, x, t) for t in (1, 0) for z, x in CHIPS]
+    far = sorted((o for o in every if 2 in o[:2]), key=lambda o: -(o[0] == 2) - (o[1] == 2))
+    near = [o for o in every if 2 not in o[:2]]
+    mixed = []
+    for i in range(max(len(far), len(near))):
+        mixed += far[i : i + 1] + near[i : i + 1]
+    return mixed + [(0, 0, 1), (0, 0, 0)]
+
+
+STEPS = steps()
 
 
 def conv_group(xp, kb, rows, pp):
@@ -165,7 +172,7 @@
     def place(k):
         core, cx = gx % 2, gx // 2
         a, b, t = (look_up(k, [o[i] for o in STEPS]) for i in range(3))
-        dy, dx = jnp.where(core == 0, a, b), jnp.where(core == 0, b, a)
+        dy, dx = jnp.where(core == 0, a, GY - b), jnp.where(core == 0, b, GX // 2 - a)
         return (gy + dy) % GY, ((cx + dx) % (GX // 2)) * 2 + (core + t) % 2
 
     def tell(k, _):

time: 97.5 us -> 94.9 us (0.973)
  Pallas kernels: 96.9 us -> 94.7 us
    pallas_call x1, Pallas kernels: 93.5 us -> 91.3 us  [per_device(): pl.pallas_call(block_kernel, out_shape=(pltpu.VMEM((N, SLOT, COLS, C), B1...]
where the time goes in v4:
time: 94.9 us; the launch traced here: 94.7 us
  Pallas kernels  94.7 us (100%)
    pallas_call x1, Pallas kernels, per_device(): pl.pallas_call(block_kernel, out_shape=(pltpu.VMEM((N, SLOT, COLS, C), B1...  91.3 us
    pallas_call x1, Pallas kernels, per_device(): pl.pallas_call(compact_kernel, out_shape=jax.ShapeDtypeStruct((RECV, COLS...  3.4 us

profile of v4, /device:TPU:1, one launch (start us, length us, event | category | flops | bytes accessed | tf_op | source)
XLA Modules:
  0.0 94.7 jit_solution(3109085424373986199)
XLA Ops:
  0.0 91.3 %shard_map.163 = (bf16[32,3,128,256]{3,2,1,0:T(8,128)(2,1)S(1)}, s32[32,1,96]{2,1,0:T(1,128)}) custom-call(s32[1,96]{1,0:T(1,128)} %sroute.1, bf16[128,128,256]{2,1,0:T(8,128)(2,1)} %x.1, s32[1,96]{1,0:T(1,128)} %sroute.1, f32[7,7,256]{2,1,0:T(8,128)} %kern.1, bf16[128,1008]{1,0:T(8,128)(2,1)} %constant.12.clone.smat_h, bf16[64,256]{1,0:T(8,128)(2,1)} %constant.13.clone.pf, ...), custom_call_target="tpu_custom_call" | custom-call | tf_op jit(solution)/shard_map/pallas_call | solution.py:319
  91.3 3.4 %shard_map.164 = bf16[48,128,256]{2,1,0:T(8,128)(2,1)} custom-call(s32[32,1,96]{2,1,0:T(1,128)} %get-tuple-element.7.routes, bf16[32,3,128,256]{3,2,1,0:T(8,128)(2,1)S(1)} %get-tuple-element.8.recv), custom_call_target="tpu_custom_call" | custom-call | tf_op jit(solution)/shard_map/pallas_call | solution.py:349

commit v5 on v4

--- a/solution.py
+++ b/solution.py
@@ -19,6 +19,7 @@
 HID = 1024
 EXT = COLS + 16
 KS = 7
+HALF = 256
 
 
 def shift_matrix():
@@ -230,45 +231,58 @@
     for h in held:
         h.wait()
 
-    def compute(k):
-        ry, rx = place(k)
-        r = ry * GX + rx
-        rows = [jnp.maximum(route[0, r * SLOT + t], 0) for t in range(SLOT)]
+    def compute(k, groups):
+        where = [place(k + i) for i in range(groups)]
+        count = groups * SLOT
+        rows = [
+            jnp.maximum(route[0, (ry * GX + rx) * SLOT + t], 0) for ry, rx in where for t in range(SLOT)
+        ]
+        conv_group(xp, kb, rows, pp)
         normed = []
-        conv_group(xp, kb, rows, pp)
-        for t in range(SLOT):
+        for t in range(count):
             d = jnp.dot(smat[...], pp[t], preferred_element_type=F32) + dbias[...]
             c = d - jnp.mean(d, axis=1, keepdims=True)
             v = jnp.mean(c * c, axis=1, keepdims=True)
             normed.append((c * lax.rsqrt(v + 1e-6) * gain[...] + nbias[...]).astype(B16))
         n = jnp.concatenate(normed, axis=0)
         branch = None
-        for q in range(4):
-            qs = slice(q * 256, (q + 1) * 256)
+        for q in range(HID // HALF):
+            qs = slice(q * HALF, (q + 1) * HALF)
             hh = jnp.dot(n, uw[:, qs], preferred_element_type=F32) + ub[:, qs]
             g = (0.5 * hh * (1.0 + lax.erf(hh * 0.7071067811865476))).astype(B16)
             part = jnp.dot(g, dw[qs, :], preferred_element_type=F32)
             branch = part if branch is None else branch + part
         branch = branch + db[...]
-        for t in range(SLOT):
+        for t in range(count):
             o = xp[rows[t] + 3, 0:COLS, :].astype(F32) + scale[...] * branch[t * COLS : (t + 1) * COLS]
-            stage[k, t] = o.astype(B16)
-        return ry, rx
-
-    def step(k, _):
-        ry, rx = compute(k)
-
-        @pl.when(k < N - 1)
+            stage[k + t // SLOT, t % SLOT] = o.astype(B16)
+        return where
+
+    def send(k, ry, rx):
+        remote(stage.at[k], recv.at[me], send_s, recv_s, dev(ry, rx)).start()
+
+    def single(k, _):
+        ((ry, rx),) = compute(k, 1)
+        send(k, ry, rx)
+        return 0
+
+    def double(j, _):
+        k = 2 * j
+        (ry, rx), (sy, sx) = compute(k, 2)
+        send(k, ry, rx)
+
+        @pl.when(k + 1 < N - 1)
         def _():
-            remote(stage.at[k], recv.at[me], send_s, recv_s, dev(ry, rx)).start()
-
-        @pl.when(k == N - 1)
+            send(k + 1, sy, sx)
+
+        @pl.when(k + 1 == N - 1)
         def _():
-            pltpu.make_async_copy(stage.at[k], recv.at[me], own_s.at[0]).start()
-
-        return 0
-
-    lax.fori_loop(0, N, step, 0)
+            pltpu.make_async_copy(stage.at[k + 1], recv.at[me], own_s.at[0]).start()
+
+        return 0
+
+    lax.fori_loop(0, 2, single, 0)
+    lax.fori_loop(1, N // 2, double, 0)
     mine.wait()
     pltpu.make_async_copy(stage.at[N - 1], recv.at[me], own_s.at[0]).wait()
     several = routes.at[pl.ds(0, N - 1)]
@@ -327,7 +341,7 @@
         scratch_shapes=[
             pltpu.VMEM((ROWS + 6, EXT, C), B16),
             pltpu.VMEM((KS * KS, 16, C), B16),
-            pltpu.VMEM((SLOT, KS * EXT, C), B16),
+            pltpu.VMEM((2 * SLOT, KS * EXT, C), B16),
             pltpu.VMEM((N, SLOT, COLS, C), B16),
             pltpu.VMEM((2, 8, 64, C), B16),
             pltpu.VMEM((2, 8, 64, C), B16),

time: 94.9 us -> 94.7 us (level)
  no operation moved by 1% of the time
where the time goes in v5:
time: 94.7 us; the launch traced here: 94.1 us
  Pallas kernels  94.1 us (99%)
    pallas_call x1, Pallas kernels, per_device(): pl.pallas_call(block_kernel, out_shape=(pltpu.VMEM((N, SLOT, COLS, C), B1...  90.7 us
    pallas_call x1, Pallas kernels, per_device(): pl.pallas_call(compact_kernel, out_shape=jax.ShapeDtypeStruct((RECV, COLS...  3.4 us

profile of v5, /device:TPU:1, one launch (start us, length us, event | category | flops | bytes accessed | tf_op | source)
XLA Modules:
  0.0 94.1 jit_solution(365426190696438999)
XLA Ops:
  0.0 90.7 %shard_map.163 = (bf16[32,3,128,256]{3,2,1,0:T(8,128)(2,1)S(1)}, s32[32,1,96]{2,1,0:T(1,128)}) custom-call(s32[1,96]{1,0:T(1,128)} %sroute.1, bf16[128,128,256]{2,1,0:T(8,128)(2,1)} %x.1, s32[1,96]{1,0:T(1,128)} %sroute.1, f32[7,7,256]{2,1,0:T(8,128)} %kern.1, bf16[128,1008]{1,0:T(8,128)(2,1)} %constant.12.clone.smat_h, bf16[64,256]{1,0:T(8,128)(2,1)} %constant.13.clone.pf, ...), custom_call_target="tpu_custom_call" | custom-call | tf_op jit(solution)/shard_map/pallas_call | solution.py:333
  90.7 3.4 %shard_map.164 = bf16[48,128,256]{2,1,0:T(8,128)(2,1)} custom-call(s32[32,1,96]{2,1,0:T(1,128)} %get-tuple-element.7.routes, bf16[32,3,128,256]{3,2,1,0:T(8,128)(2,1)S(1)} %get-tuple-element.8.recv), custom_call_target="tpu_custom_call" | custom-call | tf_op jit(solution)/shard_map/pallas_call | solution.py:363
